TPU v7x, 128 devices: a whole 4x4x4 slice. The times are simulated.
128 devices in a mesh: ctx: 32 (over z_lo, x, y), tp: 4 (over z_hi, core).
Axes of the slice: x: 4, y: 4, z: 4 (z_hi: 2, z_lo: 2; z = z_hi * 2 + z_lo), core: 2. Of those that a mesh axis runs over, the one named last changes fastest.
Arguments:
- queries: bfloat16 [8192, 4096], P('ctx', 'tp'), may hold values from -6 to 6
- attn_keys: bfloat16 [8192, 4096], P('ctx', 'tp'), may hold values from -6 to 6
- attn_values: bfloat16 [8192, 4096], P('ctx', 'tp'), may hold values from -6 to 6
- out_proj: bfloat16 [4096, 8192], P('tp'), may hold values from -0.25 to 0.25
Outputs:
- mixed: bfloat16 [8192, 8192], P('ctx', 'tp')
All inputs are finite; a program needn't handle non-finite values.
Results may differ from a plain program's by a relative error of at most 0.013.
Values may be sent and summed in bfloat16 or wider, within the bound.
A program may use at most 256 MiB of HBM per device.

v0:
```python
import jax
import jax.numpy as jnp
from jax import lax
from jax.sharding import PartitionSpec as P

HS = 128


def attend(carry, query_set, query_pos, key_piece, value_piece, key_pos):
    run_max, run_sum, run_acc = carry
    pieces = key_piece.shape[0]
    heads_local = query_set.shape[1]
    key_heads = key_piece.reshape(pieces, heads_local, HS)
    value_heads = value_piece.reshape(pieces, heads_local, HS)
    scores = jnp.einsum("rhd,phd->hrp", query_set, key_heads, preferred_element_type=jnp.float32)
    scores = scores * (1.0 / HS**0.5)
    visible = key_pos[None, None, :] <= query_pos[None, :, None]
    scores = jnp.where(visible, scores, -1e30)
    new_max = jnp.maximum(run_max, jnp.max(scores, axis=2))
    weights = jnp.where(visible, jnp.exp(scores - new_max[:, :, None]), 0.0)
    new_sum = jnp.sum(weights, axis=2)
    update = jnp.einsum(
        "hrp,phd->rhd",
        weights.astype(jnp.bfloat16),
        value_heads,
        preferred_element_type=jnp.float32,
    )
    return (new_max, new_sum, update)


def start_carry(heads_local, rows_count):
    return (
        jnp.full((heads_local, rows_count), -1e30, jnp.float32),
        jnp.zeros((heads_local, rows_count), jnp.float32),
        jnp.zeros((rows_count, heads_local, HS), jnp.float32),
    )


def body(queries, attn_keys, attn_values, out_proj):
    ctx_count = lax.axis_size("ctx")
    ctx_index = lax.axis_index("ctx")
    tok_dev = queries.shape[0]
    half_len = tok_dev // 2
    heads_local = queries.shape[1] // HS
    query_heads = queries.reshape(tok_dev, heads_local, HS)
    offsets = jnp.arange(half_len, dtype=jnp.int32)
    query_pos = jnp.concatenate(
        [ctx_index * half_len + offsets, (2 * ctx_count - 1 - ctx_index) * half_len + offsets]
    )
    key_piece = lax.all_gather(attn_keys, "ctx", axis=0, tiled=True)
    value_piece = lax.all_gather(attn_values, "ctx", axis=0, tiled=True)
    stored = jnp.arange(key_piece.shape[0], dtype=jnp.int32)
    device = stored // tok_dev
    within = stored % tok_dev
    key_pos = jnp.where(
        within < half_len,
        device * half_len + within,
        (2 * ctx_count - 1 - device) * half_len + within - half_len,
    )
    run_max, run_sum, run_acc = attend(
        start_carry(heads_local, tok_dev), query_heads, query_pos, key_piece, value_piece, key_pos
    )
    attended = (run_acc / jnp.transpose(run_sum)[:, :, None]).reshape(tok_dev, heads_local * HS)
    attended = attended.astype(jnp.bfloat16)
    partial_value = jnp.dot(attended, out_proj, preferred_element_type=jnp.float32).astype(
        jnp.bfloat16
    )
    share = lax.psum_scatter(
        partial_value.astype(jnp.float32).astype(jnp.bfloat16),
        "tp",
        scatter_dimension=1,
        tiled=True,
    )
    return share


def solution(mesh):
    in_specs = (P("ctx", "tp"), P("ctx", "tp"), P("ctx", "tp"), P("tp", None))
    out_specs = P("ctx", "tp")
    return jax.shard_map(body, mesh=mesh, in_specs=in_specs, out_specs=out_specs, check_vma=False)
```

profile of v0, /device:TPU:1, one launch (start us, length us, event | category | flops | bytes accessed | tf_op | source)
XLA Modules:
  0.0 570.7 jit_solution(6408303022841652659)
XLA Ops:
  6.5 0.0 copy-start
  6.5 0.0 all-gather.3.cloned.1.call-start
  6.5 2.1 copy.7
  8.6 0.0 all-gather.3.cloned.1.call-update
  8.7 0.0 all-gather.5.cloned.1.call-start
  8.7 0.7 all-gather.5.cloned.1.call-update
  9.4 0.0 reduce-scatter.2.cloned.1.call-start
  9.5 1.2 broadcast_compare_fusion
  10.7 224.2 %all-gather.3.cloned.1.call-done = bf16[8192,1024]{0,1:T(8,128)(2,1)} async-done(((bf16[256,1024]{0,1:T(8,128)(2,1)}), bf16[8192,1024]{0,1:T(8,128)(2,1)}) %all-gather.3.cloned.1.call-update) | async-done | bytes 16777232 | tf_op jit(solution)/shard_map/all_gather | solution.py:50
  235.0 0.0 copy-done
  235.0 31.6 %fusion = (f32[8,256]{1,0:T(8,128)S(1)}, f32[8,256,8192]{2,1,0:T(8,128)}) fusion(pred[256,8192]{1,0:T(8,128)(4,1)S(1)} %broadcast_compare_fusion, bf16[8192,8,128]{0,2,1:T(8,128)(2,1)} %bitcast.24, bf16[256,1024]{1,0:T(8,128)(2,1)S(1)} %copy-done), kind=kOutput, calls=%fused_computation.2 | convolution fusion | flops 4345296896 | bytes 86515712 | tf_op jit(solution)/shard_map/rhd,phd->hrp/dot_general | solution.py:15
  266.6 24.2 %fusion.1 = f32[8,256]{1,0:T(8,128)S(1)} fusion(f32[8,256,8192]{2,1,0:T(8,128)} %get-tuple-element.6, f32[8,256]{1,0:T(8,128)S(1)} %broadcast_maximum_fusion, pred[256,8192]{1,0:T(8,128)(4,1)S(1)} %broadcast_compare_fusion), kind=kLoop, calls=%fused_computation.3 | loop fusion | flops 83884032 | bytes 69222400 | tf_op jit(solution)/shard_map/reduce_sum | solution.py:21
  290.8 154.4 %all-gather.5.cloned.1.call-done = bf16[8192,1024]{1,0:T(8,128)(2,1)} async-done(((bf16[256,1024]{1,0:T(8,128)(2,1)}), bf16[8192,1024]{1,0:T(8,128)(2,1)}) %all-gather.5.cloned.1.call-update) | async-done | bytes 16777232 | tf_op jit(solution)/shard_map/all_gather | solution.py:51
  445.1 21.2 %copy.10 = bf16[8192,1024]{0,1:T(8,128)(2,1)} copy(bf16[8192,1024]{1,0:T(8,128)(2,1)} %all-gather.5.cloned.1.call-done) | data formatting | bytes 33554432 | tf_op jit(solution)/shard_map/all_gather | solution.py:51
  466.3 0.0 copy-start.1
  466.3 29.6 %divide_convert_fusion = bf16[256,8,128]{0,2,1:T(8,128)(2,1)S(1)} fusion(bf16[8192,8,128]{0,2,1:T(8,128)(2,1)} %bitcast.21, f32[8,256,8192]{2,1,0:T(8,128)} %get-tuple-element.6, f32[8,256]{1,0:T(8,128)S(1)} %broadcast_maximum_fusion, pred[256,8192]{1,0:T(8,128)(4,1)S(1)} %broadcast_compare_fusion, f32[256,8]{0,1:T(8,128)S(1)} %bitcast.23), kind=kOutput, calls=%fused_computation.10 | convolution fusion | flops 4379377664 | bytes 86523904 | tf_op jit(solution)/shard_map/hrp,phd->rhd/dot_general | solution.py:22
  496.0 12.2 %convolution_convert_fusion = bf16[256,8192]{1,0:T(8,128)(2,1)} fusion(bf16[256,1024]{0,1:T(8,128)(2,1)S(1)} %bitcast.22, bf16[1024,8192]{1,0:T(8,128)(2,1)} %param.7), kind=kOutput, calls=%fused_computation.7 | convolution fusion | flops 4297064448 | bytes 21495808 | tf_op jit(solution)/shard_map/dot_general | solution.py:65
  508.2 0.0 reduce-scatter.2.cloned.1.call-update
  508.2 55.9 %reduce-scatter.2.cloned.1.call-done = bf16[256,2048]{1,0:T(8,128)(2,1)} async-done(((bf16[256,8192]{1,0:T(8,128)(2,1)}), bf16[256,2048]{1,0:T(8,128)(2,1)}) %reduce-scatter.2.cloned.1.call-update) | async-done | bytes 1048592 | tf_op jit(solution)/shard_map/reduce_scatter | solution.py:68
  564.1 0.0 copy-done.1
  (4 shorter events, 0.0 us)
Async XLA Ops:
  6.5 228.4 %copy-start = (bf16[256,1024]{1,0:T(8,128)(2,1)S(1)}, bf16[256,1024]{1,0:T(8,128)(2,1)}, u32[]{:S(2)}) copy-start(bf16[256,1024]{1,0:T(8,128)(2,1)} %param.4) | copy-start | bytes 1572868
  6.5 228.4 %all-gather.3.cloned.1.call-start = ((), (), s32[]{:S(2)}) async-start(), calls=%async_computation.1 | async-start | bytes 17301504 | tf_op jit(solution)/shard_map/all_gather | solution.py:50
  8.7 436.5 %all-gather.5.cloned.1.call-start = ((), (), s32[]{:S(2)}) async-start(), calls=%async_computation.2 | async-start | bytes 17301504 | tf_op jit(solution)/shard_map/all_gather | solution.py:51
  9.4 554.7 %reduce-scatter.2.cloned.1.call-start = ((), (), s32[]{:S(2)}) async-start(), calls=%async_computation.3 | async-start | bytes 5242880 | tf_op jit(solution)/shard_map/reduce_scatter | solution.py:68
  466.3 97.8 %copy-start.1 = (bf16[256,1024]{1,0:T(8,128)(2,1)S(1)}, bf16[256,1024]{1,0:T(8,128)(2,1)}, u32[]{:S(2)}) copy-start(bf16[256,1024]{1,0:T(8,128)(2,1)} %param.4) | copy-start | bytes 1572868
Sparse Core Ops, SparseCore 0:
  8.9 225.9 all-gather.2
  236.6 208.4 all-gather.4
  508.4 55.7 reduce-scatter.1
where the time goes:
time: 571 us
  waiting for transfers between devices  435 us (76%)
  matrix products  73.5 us (13%)
  other arithmetic  25.4 us (4%)
  local copies, waits for them, and re-layouts  23.3 us (4%)
  between operations  13.2 us (2%)
    all_gather x1, waiting for transfers between devices, body(): key_piece = lax.all_gather(attn_keys, 'ctx', axis=0, tiled=True)  224 us
    all_gather x1, waiting for transfers between devices, body(): value_piece = lax.all_gather(attn_values, 'ctx', axis=0, tiled=True)  154 us
    reduce_scatter x1, waiting for transfers between devices, body(): lax.psum_scatter(partial_value.astype(jnp.float32).astype(jnp.bfloat16),...  55.9 us
    dot_general x1, matrix products, attend(): jnp.einsum('rhd,phd->hrp', query_set, key_heads, preferred_element_type=j...  31.6 us
    dot_general x1, matrix products, attend(): jnp.einsum('hrp,phd->rhd', weights.astype(jnp.bfloat16), value_heads, pre...  29.6 us
    reduce_sum x1, other arithmetic, attend(): new_sum = jnp.sum(weights, axis=2)  24.2 us
    all_gather x1, local copies, waits for them, and re-layouts, body(): value_piece = lax.all_gather(attn_values, 'ctx', axis=0, tiled=True)  21.2 us
    dot_general x1, matrix products, body(): jnp.dot(attended, out_proj, preferred_element_type=jnp.float32)  12.2 us
  transfers between devices with their start and end apart: 3, of which 3 were waited for; matrix products, arithmetic and copies ran while one was open for 10% of the time, Pallas kernels for 0%

commit v1 on v0

v1 whole, which is shorter than its diff:
```python
import functools

import jax
import jax.numpy as jnp
from jax import lax
from jax.experimental import pallas as pl
from jax.experimental.pallas import tpu as pltpu
from jax.sharding import PartitionSpec as P

MESH = pl.DeviceIdType.MESH
HS = 128
BLK = 128
GRP = 512
SCALE = 1.4426950408889634 / HS**0.5
LOW = -1e30


def attend_kernel(
    q_in, k_in, v_in, att_out,
    qbuf, kbuf, vbuf, m_ref, l_ref, acc_ref, obuf,
    xch_send, xch_recv, ring_send, ring_recv, ret_send, ret_recv,
):
    ctx = lax.axis_index("ctx")
    tp = lax.axis_index("tp")
    core = lax.rem(tp, 2)
    z, a, b = ctx // 16, lax.rem(ctx // 4, 4), lax.rem(ctx, 4)
    r = jnp.where(core == 0, a, b)
    w = jnp.where(core == 0, b, a)

    def device(z_at, r_at, w_at):
        at = z_at * 16 + jnp.where(core == 0, r_at * 4 + w_at, w_at * 4 + r_at)
        return (at, tp)

    left = device(z, lax.rem(r + 3, 4), w)
    right = device(z, lax.rem(r + 1, 4), w)
    spread = [(dz, dw) for dz in range(2) for dw in range(4)]

    def spread_at(dz, dw):
        return lax.rem(z + dz, 2), lax.rem(w + dw, 4)

    barrier = pltpu.get_barrier_semaphore()
    for dz, dw in spread[1:]:
        z_at, w_at = spread_at(dz, dw)
        pl.semaphore_signal(barrier, inc=1, device_id=device(z_at, r, w_at), device_id_type=MESH)
    for peer in (left, right):
        pl.semaphore_signal(barrier, inc=1, device_id=peer, device_id_type=MESH)
    pl.semaphore_wait(barrier, len(spread) + 1)

    ins = (q_in, k_in, v_in)

    def exchange(kind, half):
        group = z if half == 0 else 3 - z
        slot = w if half == 0 else 3 - w
        base = group * GRP + slot * BLK
        if kind > 0:
            base = base + r * (4 * GRP)
        dst = (qbuf, kbuf, vbuf)[kind].at[pl.ds(pl.multiple_of(base, BLK), BLK), :]
        for dz, dw in spread[1:] + spread[:1]:
            z_at, w_at = spread_at(dz, dw)
            column = pl.multiple_of((z_at * 4 + w_at) * HS, HS)
            src = ins[kind].at[pl.ds(half * BLK, BLK), pl.ds(column, HS)]
            if (dz, dw) == (0, 0):
                pltpu.make_async_copy(src, dst, xch_recv.at[kind, group]).start()
            else:
                pltpu.make_async_remote_copy(
                    src_ref=src, dst_ref=dst,
                    send_sem=xch_send.at[kind, half], recv_sem=xch_recv.at[kind, group],
                    device_id=device(z_at, r, w_at), device_id_type=MESH,
                ).start()

    def exchange_sent(kind, half):
        ref = ins[kind].at[pl.ds(half * BLK, BLK), pl.ds(0, 7 * HS)]
        pltpu.make_async_copy(ref, ref, xch_send.at[kind, half]).wait()

    def chunk(buf, r_at, group):
        return buf.at[pl.ds(pl.multiple_of(r_at * (4 * GRP) + group * GRP, GRP), GRP), :]

    def exchanged(kind, group):
        buf = (qbuf, kbuf, vbuf)[kind]
        ref = chunk(buf, r if kind > 0 else 0, group)
        pltpu.make_async_copy(ref, ref, xch_recv.at[kind, group]).wait()

    def ring_copy(kind, group, way, send_at, r_at, peer):
        ref = chunk((kbuf, vbuf)[kind], r_at, group)
        return pltpu.make_async_remote_copy(
            src_ref=ref, dst_ref=ref,
            send_sem=ring_send.at[group, kind, send_at], recv_sem=ring_recv.at[group, kind, way],
            device_id=peer, device_id_type=MESH,
        )

    def ring_start(group):
        for kind in range(2):
            ring_copy(kind, group, 0, 0, r, right).start()
            ring_copy(kind, group, 1, 1, r, left).start()

    r_left, r_right, r_far = lax.rem(r + 3, 4), lax.rem(r + 1, 4), lax.rem(r + 2, 4)

    def ring_wait(kind, group, way):
        r_at = (r_left, r_right, r_far)[way]
        ref = chunk((kbuf, vbuf)[kind], r_at, group)
        pltpu.make_async_copy(ref, ref, ring_recv.at[group, kind, way]).wait()

    def ring_near(group):
        ring_wait(0, group, 0)
        ring_copy(0, group, 2, 2, r_left, right).start()
        ring_wait(1, group, 1)
        ring_copy(1, group, 2, 2, r_right, left).start()
        ring_wait(1, group, 0)
        ring_wait(0, group, 1)

    def ring_far(group):
        ring_wait(0, group, 2)
        ring_wait(1, group, 2)

    def tile(q_group, r_at, k_group, size, mask=None):
        rows = pl.ds(pl.multiple_of(q_group * GRP, GRP), GRP)
        keys = pl.ds(pl.multiple_of(r_at * (4 * GRP) + k_group * GRP, GRP), size)
        scores = lax.dot_general(
            qbuf[rows, :], kbuf[keys, :], (((1,), (1,)), ((), ())), preferred_element_type=jnp.float32
        )
        if mask is not None:
            scores = jnp.where(mask, scores, LOW)
        old = m_ref[rows, :]
        new = jnp.maximum(old, jnp.max(scores, axis=1, keepdims=True))
        m_ref[rows, :] = new
        keep = jnp.exp2((old - new) * SCALE)
        shift = new * SCALE
        weights = jnp.exp2(scores * SCALE - jnp.concatenate([shift] * (size // HS), axis=1))
        total = weights[:, :HS]
        for at in range(1, size // HS):
            total = total + weights[:, at * HS:(at + 1) * HS]
        l_ref[rows, :] = l_ref[rows, :] * keep + total
        acc_ref[rows, :] = acc_ref[rows, :] * keep + jnp.dot(
            weights.astype(jnp.bfloat16), vbuf[keys, :], preferred_element_type=jnp.float32
        )

    def own_tile(group):
        row = lax.broadcasted_iota(jnp.int32, (GRP, GRP), 0)
        column = lax.broadcasted_iota(jnp.int32, (GRP, GRP), 1)
        tile(group, r, group, GRP, column <= row)

    def other_tile(group, r_at):
        before = jnp.where((r_at < r) == (group < 2), 1, 0)

        @pl.when((core == 1) | (before == 1))
        def _():
            row = lax.broadcasted_iota(jnp.int32, (GRP, GRP), 0) // BLK
            column = lax.broadcasted_iota(jnp.int32, (GRP, GRP), 1) // BLK
            count = row * jnp.where(core == 0, 0, 1) + jnp.where(core == 0, 4, 1) * before
            tile(group, r_at, group, GRP, column < count)

    def low_keys(r_at):
        @pl.loop(2, 4)
        def _(group):
            tile(group, r_at, 0, 2 * GRP)

    def finish(group):
        rows = pl.ds(group * GRP, GRP)
        total = jnp.sum(l_ref[rows, :], axis=1, keepdims=True)
        obuf[rows, :] = (acc_ref[rows, :] / total).astype(jnp.bfloat16)
        half = group // 2
        z_at = group if half == 0 else 3 - group
        column = pl.multiple_of((z * 4 + w) * HS, HS)
        dst = att_out.at[pl.ds(half * BLK, BLK), pl.ds(column, HS)]
        for dw in (1, 2, 3, 0):
            w_at = lax.rem(w + dw, 4)
            slot = w_at if half == 0 else 3 - w_at
            src = obuf.at[pl.ds(pl.multiple_of(group * GRP + slot * BLK, BLK), BLK), :]

            def remote(src=src, w_at=w_at, dw=dw):
                return pltpu.make_async_remote_copy(
                    src_ref=src, dst_ref=dst,
                    send_sem=ret_send.at[group, dw], recv_sem=ret_recv.at[half],
                    device_id=device(z_at, r, w_at), device_id_type=MESH,
                )

            if dw == 0:
                @pl.when(z == z_at)
                def _():
                    pltpu.make_async_copy(src, dst, ret_recv.at[half]).start()

                @pl.when(z != z_at)
                def _():
                    remote().start()
            else:
                remote().start()

    def returned_sent(group):
        half = group // 2
        z_at = group if half == 0 else 3 - group
        for dw in range(4):
            ref = obuf.at[pl.ds(0, BLK), :]
            if dw == 0:
                @pl.when(z != z_at)
                def _():
                    pltpu.make_async_copy(ref, ref, ret_send.at[group, dw]).wait()
            else:
                pltpu.make_async_copy(ref, ref, ret_send.at[group, dw]).wait()

    exchange(1, 0)
    exchange(2, 0)
    exchange(0, 0)
    exchange(0, 1)
    exchange(1, 1)
    exchange(2, 1)

    m_ref[...] = jnp.full_like(m_ref, LOW)
    l_ref[...] = jnp.zeros_like(l_ref)
    acc_ref[...] = jnp.zeros_like(acc_ref)

    for group in (0, 1):
        exchanged(1, group)
        exchanged(2, group)
        ring_start(group)
    exchanged(0, 0)
    exchanged(0, 1)
    own_tile(0)
    tile(1, r, 0, GRP)
    own_tile(1)
    exchanged(0, 2)
    exchanged(0, 3)
    for group in (2, 3):
        exchanged(1, group)
        exchanged(2, group)
        ring_start(group)
    low_keys(r)
    ring_near(0)
    ring_near(1)
    own_tile(2)
    tile(3, r, 2, GRP)
    own_tile(3)

    def low(r_at):
        other_tile(0, r_at)
        tile(1, r_at, 0, GRP)
        other_tile(1, r_at)
        low_keys(r_at)

    @pl.loop(0, 2)
    def _(at):
        low(lax.rem(r + 3 + 2 * at, 4))

    ring_near(2)
    ring_near(3)
    ring_far(0)
    ring_far(1)
    low(r_far)
    finish(0)
    finish(1)

    @pl.loop(0, 2)
    def _(at):
        r_at = lax.rem(r + 3 + 2 * at, 4)
        other_tile(2, r_at)
        tile(3, r_at, 2, GRP)

    ring_far(2)
    other_tile(2, r_far)
    finish(2)
    tile(3, r_far, 2, GRP)

    @pl.loop(0, 2)
    def _(at):
        other_tile(3, lax.rem(r + 3 + 2 * at, 4))

    ring_far(3)
    other_tile(3, r_far)
    finish(3)

    for half in range(2):
        ref = att_out.at[pl.ds(half * BLK, BLK), :]
        pltpu.make_async_copy(ref, ref, ret_recv.at[half]).wait()
    for kind in range(3):
        for half in range(2):
            exchange_sent(kind, half)
    for group in range(4):
        returned_sent(group)
        for kind in range(2):
            for at in range(3):
                ref = chunk(kbuf, 0, group)
                pltpu.make_async_copy(ref, ref, ring_send.at[group, kind, at]).wait()


def body(queries, attn_keys, attn_values, out_proj):
    tokens, inner = queries.shape
    any_spec = pl.BlockSpec(memory_space=pl.ANY)
    attended = pl.pallas_call(
        attend_kernel,
        out_shape=jax.ShapeDtypeStruct((tokens, inner), jnp.bfloat16),
        in_specs=[any_spec] * 3,
        out_specs=any_spec,
        scratch_shapes=[
            pltpu.VMEM((4 * GRP, HS), jnp.bfloat16),
            pltpu.VMEM((16 * GRP, HS), jnp.bfloat16),
            pltpu.VMEM((16 * GRP, HS), jnp.bfloat16),
            pltpu.VMEM((4 * GRP, HS), jnp.float32),
            pltpu.VMEM((4 * GRP, HS), jnp.float32),
            pltpu.VMEM((4 * GRP, HS), jnp.float32),
            pltpu.VMEM((4 * GRP, HS), jnp.bfloat16),
            pltpu.SemaphoreType.DMA((3, 2)),
            pltpu.SemaphoreType.DMA((3, 4)),
            pltpu.SemaphoreType.DMA((4, 2, 3)),
            pltpu.SemaphoreType.DMA((4, 2, 3)),
            pltpu.SemaphoreType.DMA((4, 4)),
            pltpu.SemaphoreType.DMA((2,)),
        ],
        compiler_params=pltpu.CompilerParams(
            collective_id=0, has_side_effects=True, vmem_limit_bytes=48 * 2**20
        ),
    )(queries, attn_keys, attn_values)
    partial_value = jnp.dot(attended, out_proj, preferred_element_type=jnp.float32).astype(jnp.bfloat16)
    return lax.psum_scatter(partial_value, "tp", scatter_dimension=1, tiled=True)


def solution(mesh):
    in_specs = (P("ctx", "tp"), P("ctx", "tp"), P("ctx", "tp"), P("tp", None))
    out_specs = P("ctx", "tp")
    return jax.shard_map(body, mesh=mesh, in_specs=in_specs, out_specs=out_specs, check_vma=False)
```

time: 571 us -> 134 us (0.23)
  waiting for transfers between devices: 435 us -> 50.8 us
  matrix products: 73.5 us -> 11.8 us
  Pallas kernels: 0 us -> 54.2 us
  other arithmetic: 25.4 us -> 0 us
  local copies, waits for them, and re-layouts: 23.3 us -> 3.12 us
    all_gather x2 -> x0, waiting for transfers between devices: 379 us -> none  [the longest x1 224 us: body(): key_piece = lax.all_gather(attn_keys, 'ctx', axis=0, tiled=True)]
    dot_general x2 -> x0, matrix products: 61.2 us -> none  [the longest x1 31.6 us: attend(): jnp.einsum('rhd,phd->hrp', query_set, key_heads, preferred_element_type=j...]
    pallas_call x0 -> x1, Pallas kernels: none -> 54.2 us  [body(): pl.pallas_call(attend_kernel, out_shape=jax.ShapeDtypeStruct((tokens, inn...]
    reduce_sum x1 -> x0, other arithmetic: 24.2 us -> none  [attend(): new_sum = jnp.sum(weights, axis=2)]
    all_gather x1 -> x0, local copies, waits for them, and re-layouts: 21.2 us -> none  [body(): value_piece = lax.all_gather(attn_values, 'ctx', axis=0, tiled=True)]
  transfers between devices with their start and end apart: 3 -> 1, of which waited for: 3 -> 1; matrix products, arithmetic and copies ran while one was open for 10% -> 0% of each run, Pallas kernels for 0% -> 0%
where the time goes in v1:
time: 134 us; the launch traced here: 133 us
  Pallas kernels  54.2 us (40%)
  waiting for transfers between devices  50.8 us (38%)
  between operations  13.4 us (10%)
  matrix products  11.8 us (9%)
  local copies, waits for them, and re-layouts  3.12 us (2%)
    pallas_call x1, Pallas kernels, body(): pl.pallas_call(attend_kernel, out_shape=jax.ShapeDtypeStruct((tokens, inn...  54.2 us
    reduce_scatter x1, waiting for transfers between devices, body(): lax.psum_scatter(partial_value, 'tp', scatter_dimension=1, tiled=True)  50.8 us
    dot_general x1, matrix products, body(): jnp.dot(attended, out_proj, preferred_element_type=jnp.float32)  11.8 us
    unnamed x6, local copies, waits for them, and re-layouts  3.12 us
  transfers between devices with their start and end apart: 1, of which 1 were waited for; matrix products, arithmetic and copies ran while one was open for 0% of the time, Pallas kernels for 0%

profile of v1, /device:TPU:1, one launch (start us, length us, event | category | flops | bytes accessed | tf_op | source)
XLA Modules:
  0.0 133.3 jit_solution(7995433462158270774)
XLA Ops:
  6.5 0.0 reduce-scatter.2.cloned.1.call-start
  6.5 0.0 copy-start
  6.5 1.0 copy-done
  7.6 0.0 copy-start.1
  7.6 1.0 copy-done.1
  8.6 0.0 copy-start.2
  8.6 1.0 copy-done.2
  9.7 54.2 %shard_map.46 = bf16[256,1024]{1,0:T(8,128)(2,1)S(1)} custom-call(bf16[256,1024]{1,0:T(8,128)(2,1)S(1)} %copy-done, bf16[256,1024]{1,0:T(8,128)(2,1)S(1)} %copy-done.1, bf16[256,1024]{1,0:T(8,128)(2,1)S(1)} %copy-done.2), custom_call_target="tpu_custom_call" | custom-call | tf_op jit(solution)/shard_map/pallas_call | solution.py:287
  63.9 11.8 %convolution_convert_fusion = bf16[256,8192]{1,0:T(8,128)(2,1)} fusion(bf16[256,1024]{1,0:T(8,128)(2,1)S(1)} %shard_map.46, bf16[1024,8192]{1,0:T(8,128)(2,1)} %param.7), kind=kOutput, calls=%fused_computation | convolution fusion | flops 4297064448 | bytes 21495808 | tf_op jit(solution)/shard_map/dot_general | solution.py:311
  75.7 0.0 reduce-scatter.2.cloned.1.call-update
  75.7 50.8 %reduce-scatter.2.cloned.1.call-done = bf16[256,2048]{1,0:T(8,128)(2,1)} async-done(((bf16[256,8192]{1,0:T(8,128)(2,1)}), bf16[256,2048]{1,0:T(8,128)(2,1)}) %reduce-scatter.2.cloned.1.call-update) | async-done | bytes 1048592 | tf_op jit(solution)/shard_map/reduce_scatter | solution.py:312
Async XLA Ops:
  6.5 120.0 %reduce-scatter.2.cloned.1.call-start = ((), (), s32[]{:S(2)}) async-start(), calls=%async_computation.1 | async-start | bytes 5242880 | tf_op jit(solution)/shard_map/reduce_scatter | solution.py:312
  6.5 1.0 copy-start
  7.6 1.0 copy-start.1
  8.6 1.0 copy-start.2
Sparse Core Ops, SparseCore 0:
  75.8 50.5 reduce-scatter.1

commit v2 on v1

--- a/solution.py
+++ b/solution.py
@@ -13,12 +13,16 @@
 GRP = 512
 SCALE = 1.4426950408889634 / HS**0.5
 LOW = -1e30
-
-
-def attend_kernel(
-    q_in, k_in, v_in, att_out,
-    qbuf, kbuf, vbuf, m_ref, l_ref, acc_ref, obuf,
+OUT = 2048
+PIECE = 1024
+PIECES = OUT // PIECE
+
+
+def block_kernel(
+    q_in, k_in, v_in, w_in, out_ref,
+    qbuf, kbuf, vbuf, m_ref, l_ref, acc_ref, obuf, att, wbuf, give, got, far_give, far_got, home,
     xch_send, xch_recv, ring_send, ring_recv, ret_send, ret_recv,
+    give_send, give_recv, far_send, far_recv, w_sem,
 ):
     ctx = lax.axis_index("ctx")
     tp = lax.axis_index("tp")
@@ -44,7 +48,11 @@
         pl.semaphore_signal(barrier, inc=1, device_id=device(z_at, r, w_at), device_id_type=MESH)
     for peer in (left, right):
         pl.semaphore_signal(barrier, inc=1, device_id=peer, device_id_type=MESH)
-    pl.semaphore_wait(barrier, len(spread) + 1)
+    twin = (ctx, tp + 1 - 2 * core)
+    far = (ctx, lax.rem(tp + 2, 4))
+    for peer in (twin, far):
+        pl.semaphore_signal(barrier, inc=1, device_id=peer, device_id_type=MESH)
+    pl.semaphore_wait(barrier, len(spread) + 3)
 
     ins = (q_in, k_in, v_in)
 
@@ -161,7 +169,7 @@
         half = group // 2
         z_at = group if half == 0 else 3 - group
         column = pl.multiple_of((z * 4 + w) * HS, HS)
-        dst = att_out.at[pl.ds(half * BLK, BLK), pl.ds(column, HS)]
+        dst = att.at[pl.ds(half * BLK, BLK), pl.ds(column, HS)]
         for dw in (1, 2, 3, 0):
             w_at = lax.rem(w + dw, 4)
             slot = w_at if half == 0 else 3 - w_at
@@ -197,16 +205,82 @@
             else:
                 pltpu.make_async_copy(ref, ref, ret_send.at[group, dw]).wait()
 
+    def project(half, tp_at, at):
+        column = pl.multiple_of(tp_at * OUT + at * PIECE, PIECE)
+        return jnp.dot(
+            att[pl.ds(half * BLK, BLK), :], wbuf[:, pl.ds(column, PIECE)], preferred_element_type=jnp.float32
+        )
+
+    def piece(buf, *lead):
+        *lead, at = lead
+        return buf.at[(*lead, slice(None), pl.ds(pl.multiple_of(at * PIECE, PIECE), PIECE))]
+
+    def give_copy(half, which, at):
+        return pltpu.make_async_remote_copy(
+            src_ref=piece(give, half, which, at), dst_ref=piece(got, half, which, at),
+            send_sem=give_send.at[half, which, at], recv_sem=give_recv.at[half, which, at],
+            device_id=twin, device_id_type=MESH,
+        )
+
+    def far_copy(half, at):
+        return pltpu.make_async_remote_copy(
+            src_ref=piece(far_give, half, at), dst_ref=piece(far_got, half, at),
+            send_sem=far_send.at[half, at], recv_sem=far_recv.at[half, at],
+            device_id=far, device_id_type=MESH,
+        )
+
+    def project_give(half, which):
+        tp_at = lax.rem(twin[1] + (2 if which == 0 else 0), 4)
+
+        @pl.loop(0, PIECES)
+        def _(at):
+            piece(give, half, which, at)[...] = project(half, tp_at, at).astype(jnp.bfloat16)
+            give_copy(half, which, at).start()
+
+    def project_far(half):
+        @pl.loop(0, PIECES)
+        def _(at):
+            own = project(half, far[1], at)
+            give_copy(half, 0, at).wait_recv()
+            piece(far_give, half, at)[...] = (own + piece(got, half, 0, at)[...].astype(jnp.float32)).astype(jnp.bfloat16)
+            far_copy(half, at).start()
+
+    def project_home(half):
+        @pl.loop(0, PIECES)
+        def _(at):
+            own = project(half, tp, at)
+            give_copy(half, 1, at).wait_recv()
+            piece(home, half, at)[...] = own + piece(got, half, 1, at)[...].astype(jnp.float32)
+
+    def project_end(half):
+        @pl.loop(0, PIECES)
+        def _(at):
+            far_copy(half, at).wait_recv()
+            both = piece(home, half, at)[...] + piece(far_got, half, at)[...].astype(jnp.float32)
+            columns = pl.ds(pl.multiple_of(at * PIECE, PIECE), PIECE)
+            out_ref[pl.ds(half * BLK, BLK), columns] = both.astype(jnp.bfloat16)
+
+    def returned(half):
+        ref = att.at[pl.ds(half * BLK, BLK), :]
+        pltpu.make_async_copy(ref, ref, ret_recv.at[half]).wait()
+
     exchange(1, 0)
     exchange(2, 0)
     exchange(0, 0)
     exchange(0, 1)
     exchange(1, 1)
     exchange(2, 1)
+    load_w = pltpu.make_async_copy(w_in, wbuf, w_sem)
+    load_w.start()
 
     m_ref[...] = jnp.full_like(m_ref, LOW)
     l_ref[...] = jnp.zeros_like(l_ref)
     acc_ref[...] = jnp.zeros_like(acc_ref)
+
+    def low(r_at):
+        other_tile(0, r_at)
+        tile(1, r_at, 0, GRP)
+        other_tile(1, r_at)
 
     for group in (0, 1):
         exchanged(1, group)
@@ -219,34 +293,37 @@
     own_tile(1)
     exchanged(0, 2)
     exchanged(0, 3)
+    ring_near(0)
+    low_keys(r)
+    ring_near(1)
     for group in (2, 3):
         exchanged(1, group)
         exchanged(2, group)
         ring_start(group)
-    low_keys(r)
-    ring_near(0)
-    ring_near(1)
-    own_tile(2)
-    tile(3, r, 2, GRP)
-    own_tile(3)
-
-    def low(r_at):
-        other_tile(0, r_at)
-        tile(1, r_at, 0, GRP)
-        other_tile(1, r_at)
-        low_keys(r_at)
 
     @pl.loop(0, 2)
     def _(at):
         low(lax.rem(r + 3 + 2 * at, 4))
 
-    ring_near(2)
-    ring_near(3)
+    low_keys(r_left)
     ring_far(0)
     ring_far(1)
     low(r_far)
     finish(0)
     finish(1)
+    low_keys(r_right)
+    ring_near(2)
+    ring_near(3)
+    low_keys(r_far)
+    load_w.wait()
+    returned(0)
+    project_give(0, 0)
+    project_far(0)
+    project_give(0, 1)
+    project_home(0)
+    own_tile(2)
+    tile(3, r, 2, GRP)
+    own_tile(3)
 
     @pl.loop(0, 2)
     def _(at):
@@ -266,10 +343,14 @@
     ring_far(3)
     other_tile(3, r_far)
     finish(3)
-
-    for half in range(2):
-        ref = att_out.at[pl.ds(half * BLK, BLK), :]
-        pltpu.make_async_copy(ref, ref, ret_recv.at[half]).wait()
+    project_end(0)
+    returned(1)
+    project_give(1, 0)
+    project_far(1)
+    project_give(1, 1)
+    project_home(1)
+    project_end(1)
+
     for kind in range(3):
         for half in range(2):
             exchange_sent(kind, half)
@@ -279,16 +360,21 @@
             for at in range(3):
                 ref = chunk(kbuf, 0, group)
                 pltpu.make_async_copy(ref, ref, ring_send.at[group, kind, at]).wait()
+    for half in range(2):
+        for at in range(PIECES):
+            give_copy(half, 0, at).wait_send()
+            give_copy(half, 1, at).wait_send()
+            far_copy(half, at).wait_send()
 
 
 def body(queries, attn_keys, attn_values, out_proj):
     tokens, inner = queries.shape
     any_spec = pl.BlockSpec(memory_space=pl.ANY)
-    attended = pl.pallas_call(
-        attend_kernel,
-        out_shape=jax.ShapeDtypeStruct((tokens, inner), jnp.bfloat16),
-        in_specs=[any_spec] * 3,
-        out_specs=any_spec,
+    return pl.pallas_call(
+        block_kernel,
+        out_shape=jax.ShapeDtypeStruct((tokens, OUT), jnp.bfloat16),
+        in_specs=[any_spec] * 4,
+        out_specs=pl.BlockSpec(memory_space=pltpu.VMEM),
         scratch_shapes=[
             pltpu.VMEM((4 * GRP, HS), jnp.bfloat16),
             pltpu.VMEM((16 * GRP, HS), jnp.bfloat16),
@@ -297,19 +383,29 @@
             pltpu.VMEM((4 * GRP, HS), jnp.float32),
             pltpu.VMEM((4 * GRP, HS), jnp.float32),
             pltpu.VMEM((4 * GRP, HS), jnp.bfloat16),
+            pltpu.VMEM((tokens, inner), jnp.bfloat16),
+            pltpu.VMEM((inner, 4 * OUT), jnp.bfloat16),
+            pltpu.VMEM((2, 2, BLK, OUT), jnp.bfloat16),
+            pltpu.VMEM((2, 2, BLK, OUT), jnp.bfloat16),
+            pltpu.VMEM((2, BLK, OUT), jnp.bfloat16),
+            pltpu.VMEM((2, BLK, OUT), jnp.bfloat16),
+            pltpu.VMEM((2, BLK, OUT), jnp.float32),
             pltpu.SemaphoreType.DMA((3, 2)),
             pltpu.SemaphoreType.DMA((3, 4)),
             pltpu.SemaphoreType.DMA((4, 2, 3)),
             pltpu.SemaphoreType.DMA((4, 2, 3)),
             pltpu.SemaphoreType.DMA((4, 4)),
             pltpu.SemaphoreType.DMA((2,)),
+            pltpu.SemaphoreType.DMA((2, 2, PIECES)),
+            pltpu.SemaphoreType.DMA((2, 2, PIECES)),
+            pltpu.SemaphoreType.DMA((2, PIECES)),
+            pltpu.SemaphoreType.DMA((2, PIECES)),
+            pltpu.SemaphoreType.DMA,
         ],
         compiler_params=pltpu.CompilerParams(
-            collective_id=0, has_side_effects=True, vmem_limit_bytes=48 * 2**20
+            collective_id=0, has_side_effects=True, vmem_limit_bytes=60 * 2**20
         ),
-    )(queries, attn_keys, attn_values)
-    partial_value = jnp.dot(attended, out_proj, preferred_element_type=jnp.float32).astype(jnp.bfloat16)
-    return lax.psum_scatter(partial_value, "tp", scatter_dimension=1, tiled=True)
+    )(queries, attn_keys, attn_values, out_proj)
 
 
 def solution(mesh):

time: 134 us -> 84.3 us (0.63)
  waiting for transfers between devices: 50.8 us -> 0 us
  Pallas kernels: 54.2 us -> 81.8 us
  between operations: 13.4 us -> 0.01 us
  matrix products: 11.8 us -> 0 us
    reduce_scatter x1 -> x0, waiting for transfers between devices: 50.8 us -> none  [body(): lax.psum_scatter(partial_value, 'tp', scatter_dimension=1, tiled=True)]
    pallas_call x1, Pallas kernels: 54.2 us -> 81.8 us  [body(): pl.pallas_call(block_kernel, out_shape=jax.ShapeDtypeStruct((tokens, OUT)...]
    dot_general x1 -> x0, matrix products: 11.8 us -> none  [body(): jnp.dot(attended, out_proj, preferred_element_type=jnp.float32)]
    unnamed x6 -> x1, local copies, waits for them, and re-layouts: 3.12 us -> 2.3 us
  transfers between devices with their start and end apart: 1 -> 0, of which waited for: 1 -> 0; matrix products, arithmetic and copies ran while one was open for 0% -> 0% of each run, Pallas kernels for 0% -> 0%
where the time goes in v2:
time: 84.3 us; the launch traced here: 84.2 us
  Pallas kernels  81.8 us (97%)
  local copies, waits for them, and re-layouts  2.3 us (3%)
    pallas_call x1, Pallas kernels, body(): pl.pallas_call(block_kernel, out_shape=jax.ShapeDtypeStruct((tokens, OUT)...  81.8 us
    unnamed x1, local copies, waits for them, and re-layouts  2.3 us

profile of v2, /device:TPU:1, one launch (start us, length us, event | category | flops | bytes accessed | tf_op | source)
XLA Modules:
  0.0 84.2 jit_solution(7011584864676163958)
XLA Ops:
  0.0 81.8 %shard_map.46 = bf16[256,2048]{1,0:T(8,128)(2,1)} custom-call(bf16[256,1024]{1,0:T(8,128)(2,1)} %q_in.1, bf16[256,1024]{1,0:T(8,128)(2,1)} %k_in.1, bf16[256,1024]{1,0:T(8,128)(2,1)} %v_in.1, bf16[1024,8192]{1,0:T(8,128)(2,1)} %w_in.1), custom_call_target="tpu_custom_call" | custom-call | tf_op jit(solution)/shard_map/pallas_call | solution.py:373
  81.8 2.3 %copy.6 = bf16[256,2048]{1,0:T(8,128)(2,1)} copy(bf16[256,2048]{1,0:T(8,128)(2,1)} %shard_map.46) | data formatting | bytes 2097152

commit v3 on v2

--- a/solution.py
+++ b/solution.py
@@ -63,7 +63,7 @@
         if kind > 0:
             base = base + r * (4 * GRP)
         dst = (qbuf, kbuf, vbuf)[kind].at[pl.ds(pl.multiple_of(base, BLK), BLK), :]
-        for dz, dw in spread[1:] + spread[:1]:
+        for dz, dw in spread[4:] + spread[1:4] + spread[:1]:
             z_at, w_at = spread_at(dz, dw)
             column = pl.multiple_of((z_at * 4 + w_at) * HS, HS)
             src = ins[kind].at[pl.ds(half * BLK, BLK), pl.ds(column, HS)]
@@ -120,8 +120,8 @@
         ring_wait(0, group, 2)
         ring_wait(1, group, 2)
 
-    def tile(q_group, r_at, k_group, size, mask=None):
-        rows = pl.ds(pl.multiple_of(q_group * GRP, GRP), GRP)
+    def tile(q_group, r_at, k_group, size, mask=None, tall=1):
+        rows = pl.ds(pl.multiple_of(q_group * GRP, GRP), tall * GRP)
         keys = pl.ds(pl.multiple_of(r_at * (4 * GRP) + k_group * GRP, GRP), size)
         scores = lax.dot_general(
             qbuf[rows, :], kbuf[keys, :], (((1,), (1,)), ((), ())), preferred_element_type=jnp.float32
@@ -158,9 +158,7 @@
             tile(group, r_at, group, GRP, column < count)
 
     def low_keys(r_at):
-        @pl.loop(2, 4)
-        def _(group):
-            tile(group, r_at, 0, 2 * GRP)
+        tile(2, r_at, 0, 2 * GRP, tall=2)
 
     def finish(group):
         rows = pl.ds(group * GRP, GRP)
@@ -266,82 +264,87 @@
 
     exchange(1, 0)
     exchange(2, 0)
-    exchange(0, 0)
-    exchange(0, 1)
-    exchange(1, 1)
-    exchange(2, 1)
     load_w = pltpu.make_async_copy(w_in, wbuf, w_sem)
     load_w.start()
 
     m_ref[...] = jnp.full_like(m_ref, LOW)
     l_ref[...] = jnp.zeros_like(l_ref)
     acc_ref[...] = jnp.zeros_like(acc_ref)
+
+    def exchanged_start(group):
+        exchanged(1, group)
+        exchanged(2, group)
+        ring_start(group)
 
     def low(r_at):
         other_tile(0, r_at)
         tile(1, r_at, 0, GRP)
         other_tile(1, r_at)
 
-    for group in (0, 1):
-        exchanged(1, group)
-        exchanged(2, group)
-        ring_start(group)
+    def high(r_at):
+        other_tile(2, r_at)
+        tile(3, r_at, 2, GRP)
+        other_tile(3, r_at)
+
+    first, second, third, fourth = z, 1 - z, 3 - z, 2 + z
+
+    exchanged_start(first)
+    exchange(0, 0)
+    exchanged_start(second)
+    exchange(1, 1)
+    exchange(2, 1)
     exchanged(0, 0)
     exchanged(0, 1)
+    exchange(0, 1)
     own_tile(0)
     tile(1, r, 0, GRP)
     own_tile(1)
-    exchanged(0, 2)
-    exchanged(0, 3)
-    ring_near(0)
-    low_keys(r)
-    ring_near(1)
-    for group in (2, 3):
-        exchanged(1, group)
-        exchanged(2, group)
-        ring_start(group)
+    ring_near(first)
+    ring_near(second)
+    exchanged_start(third)
 
     @pl.loop(0, 2)
     def _(at):
         low(lax.rem(r + 3 + 2 * at, 4))
 
-    low_keys(r_left)
-    ring_far(0)
-    ring_far(1)
+    exchanged_start(fourth)
+    ring_far(first)
+    ring_far(second)
     low(r_far)
     finish(0)
     finish(1)
-    low_keys(r_right)
-    ring_near(2)
-    ring_near(3)
-    low_keys(r_far)
+    exchanged(0, 2)
+    exchanged(0, 3)
+
+    @pl.loop(0, 2)
+    def _(at):
+        low_keys(lax.rem(r + 3 * at, 4))
+
+    ring_near(third)
+
+    @pl.loop(0, 2)
+    def _(at):
+        low_keys(lax.rem(r + 1 + at, 4))
+
+    ring_near(fourth)
     load_w.wait()
     returned(0)
     project_give(0, 0)
     project_far(0)
-    project_give(0, 1)
-    project_home(0)
     own_tile(2)
     tile(3, r, 2, GRP)
     own_tile(3)
 
     @pl.loop(0, 2)
     def _(at):
-        r_at = lax.rem(r + 3 + 2 * at, 4)
-        other_tile(2, r_at)
-        tile(3, r_at, 2, GRP)
-
-    ring_far(2)
-    other_tile(2, r_far)
+        high(lax.rem(r + 3 + 2 * at, 4))
+
+    project_give(0, 1)
+    project_home(0)
+    ring_far(third)
+    ring_far(fourth)
+    high(r_far)
     finish(2)
-    tile(3, r_far, 2, GRP)
-
-    @pl.loop(0, 2)
-    def _(at):
-        other_tile(3, lax.rem(r + 3 + 2 * at, 4))
-
-    ring_far(3)
-    other_tile(3, r_far)
     finish(3)
     project_end(0)
     returned(1)

time: 84.3 us -> 77.9 us (0.924)
  Pallas kernels: 81.8 us -> 75.4 us
    pallas_call x1, Pallas kernels: 81.8 us -> 75.4 us  [body(): pl.pallas_call(block_kernel, out_shape=jax.ShapeDtypeStruct((tokens, OUT)...]
where the time goes in v3:
time: 77.9 us; the launch traced here: 77.7 us
  Pallas kernels  75.4 us (97%)
  local copies, waits for them, and re-layouts  2.3 us (3%)
    pallas_call x1, Pallas kernels, body(): pl.pallas_call(block_kernel, out_shape=jax.ShapeDtypeStruct((tokens, OUT)...  75.4 us
    unnamed x1, local copies, waits for them, and re-layouts  2.3 us

profile of v3, /device:TPU:1, one launch (start us, length us, event | category | flops | bytes accessed | tf_op | source)
XLA Modules:
  0.0 77.7 jit_solution(16356943824221841989)
XLA Ops:
  0.0 75.4 %shard_map.46 = bf16[256,2048]{1,0:T(8,128)(2,1)} custom-call(bf16[256,1024]{1,0:T(8,128)(2,1)} %q_in.1, bf16[256,1024]{1,0:T(8,128)(2,1)} %k_in.1, bf16[256,1024]{1,0:T(8,128)(2,1)} %v_in.1, bf16[1024,8192]{1,0:T(8,128)(2,1)} %w_in.1), custom_call_target="tpu_custom_call" | custom-call | tf_op jit(solution)/shard_map/pallas_call | solution.py:376
  75.4 2.3 %copy.6 = bf16[256,2048]{1,0:T(8,128)(2,1)} copy(bf16[256,2048]{1,0:T(8,128)(2,1)} %shard_map.46) | data formatting | bytes 2097152

commit v4 on v3

--- a/solution.py
+++ b/solution.py
@@ -322,15 +322,13 @@
 
     ring_near(third)
 
-    @pl.loop(0, 2)
-    def _(at):
-        low_keys(lax.rem(r + 1 + at, 4))
-
+    low_keys(r_right)
     ring_near(fourth)
     load_w.wait()
     returned(0)
     project_give(0, 0)
     project_far(0)
+    low_keys(r_far)
     own_tile(2)
     tile(3, r, 2, GRP)
     own_tile(3)
@@ -339,19 +337,19 @@
     def _(at):
         high(lax.rem(r + 3 + 2 * at, 4))
 
-    project_give(0, 1)
-    project_home(0)
     ring_far(third)
     ring_far(fourth)
     high(r_far)
     finish(2)
     finish(3)
-    project_end(0)
+    project_give(0, 1)
+    project_home(0)
     returned(1)
     project_give(1, 0)
     project_far(1)
     project_give(1, 1)
     project_home(1)
+    project_end(0)
     project_end(1)
 
     for kind in range(3):

time: 77.9 us -> 76.8 us (0.986)
  Pallas kernels: 75.4 us -> 74.3 us
    pallas_call x1, Pallas kernels: 75.4 us -> 74.3 us  [body(): pl.pallas_call(block_kernel, out_shape=jax.ShapeDtypeStruct((tokens, OUT)...]
where the time goes in v4:
time: 76.8 us; the launch traced here: 76.6 us
  Pallas kernels  74.3 us (97%)
  local copies, waits for them, and re-layouts  2.3 us (3%)
    pallas_call x1, Pallas kernels, body(): pl.pallas_call(block_kernel, out_shape=jax.ShapeDtypeStruct((tokens, OUT)...  74.3 us
    unnamed x1, local copies, waits for them, and re-layouts  2.3 us

profile of v4, /device:TPU:1, one launch (start us, length us, event | category | flops | bytes accessed | tf_op | source)
XLA Modules:
  0.0 76.6 jit_solution(15161851002814188519)
XLA Ops:
  0.0 74.3 %shard_map.46 = bf16[256,2048]{1,0:T(8,128)(2,1)} custom-call(bf16[256,1024]{1,0:T(8,128)(2,1)} %q_in.1, bf16[256,1024]{1,0:T(8,128)(2,1)} %k_in.1, bf16[256,1024]{1,0:T(8,128)(2,1)} %v_in.1, bf16[1024,8192]{1,0:T(8,128)(2,1)} %w_in.1), custom_call_target="tpu_custom_call" | custom-call | tf_op jit(solution)/shard_map/pallas_call | solution.py:374
  74.3 2.3 %copy.6 = bf16[256,2048]{1,0:T(8,128)(2,1)} copy(bf16[256,2048]{1,0:T(8,128)(2,1)} %shard_map.46) | data formatting | bytes 2097152

commit v5 on v4

--- a/solution.py
+++ b/solution.py
@@ -52,6 +52,11 @@
     far = (ctx, lax.rem(tp + 2, 4))
     for peer in (twin, far):
         pl.semaphore_signal(barrier, inc=1, device_id=peer, device_id_type=MESH)
+    load_w = pltpu.make_async_copy(w_in, wbuf, w_sem)
+    load_w.start()
+    m_ref[...] = jnp.full_like(m_ref, LOW)
+    l_ref[...] = jnp.zeros_like(l_ref)
+    acc_ref[...] = jnp.zeros_like(acc_ref)
     pl.semaphore_wait(barrier, len(spread) + 3)
 
     ins = (q_in, k_in, v_in)
@@ -264,12 +269,6 @@
 
     exchange(1, 0)
     exchange(2, 0)
-    load_w = pltpu.make_async_copy(w_in, wbuf, w_sem)
-    load_w.start()
-
-    m_ref[...] = jnp.full_like(m_ref, LOW)
-    l_ref[...] = jnp.zeros_like(l_ref)
-    acc_ref[...] = jnp.zeros_like(acc_ref)
 
     def exchanged_start(group):
         exchanged(1, group)

time: 76.8 us -> 76.8 us (level)
  no operation moved by 1% of the time
where the time goes in v5:
time: 76.8 us; the launch traced here: 76.6 us
  Pallas kernels  74.3 us (97%)
  local copies, waits for them, and re-layouts  2.3 us (3%)
    pallas_call x1, Pallas kernels, body(): pl.pallas_call(block_kernel, out_shape=jax.ShapeDtypeStruct((tokens, OUT)...  74.3 us
    unnamed x1, local copies, waits for them, and re-layouts  2.3 us

profile of v5, /device:TPU:1, one launch (start us, length us, event | category | flops | bytes accessed | tf_op | source)
XLA Modules:
  0.0 76.6 jit_solution(10908591900124968515)
XLA Ops:
  0.0 74.3 %shard_map.46 = bf16[256,2048]{1,0:T(8,128)(2,1)} custom-call(bf16[256,1024]{1,0:T(8,128)(2,1)} %q_in.1, bf16[256,1024]{1,0:T(8,128)(2,1)} %k_in.1, bf16[256,1024]{1,0:T(8,128)(2,1)} %v_in.1, bf16[1024,8192]{1,0:T(8,128)(2,1)} %w_in.1), custom_call_target="tpu_custom_call" | custom-call | tf_op jit(solution)/shard_map/pallas_call | solution.py:373
  74.3 2.3 %copy.6 = bf16[256,2048]{1,0:T(8,128)(2,1)} copy(bf16[256,2048]{1,0:T(8,128)(2,1)} %shard_map.46) | data formatting | bytes 2097152
